TPU v7x, 256 devices: a whole 4x4x8 slice. The times are simulated.
256 devices in a mesh: wide: 64 (over x, y_hi, z), narrow: 4 (over y_lo, core).
Axes of the slice: x: 4, y: 4 (y_hi: 2, y_lo: 2; y = y_hi * 2 + y_lo), z: 8, core: 2. Of those that a mesh axis runs over, the one named last changes fastest.
Arguments:
- image_embed: float32 [16384, 1152], P(('wide', 'narrow')), as said below
- text_embed: float32 [16384, 1152], P(('wide', 'narrow')), as said below
- log_temp: float32 [1], replicated, may hold values from 2.3 to 3
- bias: float32 [1], replicated, may hold values from -11 to -9
Outputs:
- loss: float32 [1], replicated
- image_grad: float32 [16384, 1152], P(('wide', 'narrow'))
- text_grad: float32 [16384, 1152], P(('wide', 'narrow'))
- temp_grad: float32 [1], replicated
- bias_grad: float32 [1], replicated
Inputs may be any that keep to these rules, and one draw needn't show every extreme that they name: `image_embed`: rows of real numbers whose lengths differ from row to row. `text_embed`: rows of real numbers whose lengths differ from row to row.
All inputs are finite; a program needn't handle non-finite values.
Results may differ from a plain program's by a relative error of at most 0.0018.
Values may be sent and summed in bfloat16 or wider, within the bound.
A program may use at most 128 MiB of HBM per device.

v0:
```python
import jax
import jax.numpy as jnp
from jax import lax
from jax.sharding import PartitionSpec as P

EPS = 1e-06


def unit_rows(values):
    inverse = lax.rsqrt(jnp.sum(values * values, axis=1, keepdims=True) + EPS)
    return (values * inverse, inverse)


def back_rows(unit, inverse, direction):
    along = jnp.sum(unit * direction, axis=1, keepdims=True)
    return inverse * (direction - unit * along)


def pair_tile(rows_low, row_ids, text_all, text_ids, scale, offset):
    sim = lax.dot_general(
        rows_low, text_all, (((1,), (1,)), ((), ())), preferred_element_type=jnp.float32
    )
    logits = scale * sim + offset
    label = jnp.where(row_ids[:, None] == text_ids[None, :], 1.0, -1.0).astype(jnp.float32)
    loss_sum = jnp.sum(jax.nn.softplus(-label * logits))
    pair_grad = -label * jax.nn.sigmoid(-label * logits)
    temp_sum = jnp.sum(pair_grad * scale * sim)
    bias_sum = jnp.sum(pair_grad)
    pair_low = pair_grad.astype(jnp.bfloat16)
    image_dir = scale * jnp.dot(pair_low, text_all, preferred_element_type=jnp.float32)
    text_term = scale * lax.dot_general(
        pair_low, rows_low, (((0,), (0,)), ((), ())), preferred_element_type=jnp.float32
    )
    return (image_dir, text_term, loss_sum, temp_sum, bias_sum)


def whole_text_ids(wide_count, rows, narrow_count, narrow_pos):
    gathered_pos = jnp.arange(wide_count * rows, dtype=jnp.int32)
    return (gathered_pos // rows * narrow_count + narrow_pos) * rows + gathered_pos % rows


def on_device(image_embed, text_embed, log_temp, bias):
    rows = image_embed.shape[0]
    wide_count = lax.axis_size("wide")
    narrow_count = lax.axis_size("narrow")
    wide_pos = lax.axis_index("wide")
    narrow_pos = lax.axis_index("narrow")
    total = rows * wide_count * narrow_count
    image_unit, inv_image = unit_rows(image_embed)
    text_unit, inv_text = unit_rows(text_embed)
    image_low = image_unit.astype(jnp.bfloat16)
    text_low = text_unit.astype(jnp.bfloat16)
    scale = jnp.exp(log_temp[0])
    offset = bias[0]
    text_all = lax.all_gather(text_low, "wide", axis=0, tiled=True)
    text_ids = whole_text_ids(wide_count, rows, narrow_count, narrow_pos)
    image_all = lax.all_gather(image_low, "narrow", axis=0, tiled=True)
    row_ids = wide_pos * narrow_count * rows + jnp.arange(narrow_count * rows, dtype=jnp.int32)
    image_dir, text_term, loss_sum, temp_sum, bias_sum = pair_tile(
        image_all, row_ids, text_all, text_ids, scale, offset
    )
    image_dir = lax.psum_scatter(image_dir, "narrow", scatter_dimension=0, tiled=True)
    text_dir = lax.psum_scatter(text_term, "wide", scatter_dimension=0, tiled=True)
    loss_sum, temp_sum, bias_sum = lax.psum((loss_sum, temp_sum, bias_sum), ("wide", "narrow"))
    image_grad = back_rows(image_unit, inv_image, image_dir)
    text_grad = back_rows(text_unit, inv_text, text_dir)
    loss = (loss_sum / total).reshape(1)
    temp_grad = (temp_sum / total).reshape(1)
    bias_grad = (bias_sum / total).reshape(1)
    return (loss, image_grad, text_grad, temp_grad, bias_grad)


def solution(mesh):
    placed = (P(("wide", "narrow"), None), P(("wide", "narrow"), None), P(), P())
    return jax.shard_map(
        on_device,
        mesh=mesh,
        in_specs=placed,
        out_specs=(P(), P(("wide", "narrow"), None), P(("wide", "narrow"), None), P(), P()),
        check_vma=False,
    )
```

profile of v0, /device:TPU:1, one launch (start us, length us, event | category | flops | bytes accessed | tf_op | source)
XLA Modules:
  0.0 1090.2 jit_solution(15929786006545381309)
XLA Ops:
  7.2 0.0 all-gather.2.cloned.1.call-start
  7.2 1.1 multiply_reduce_fusion.3
  8.3 1.7 multiply_convert_fusion
  10.0 0.0 all-gather.2.cloned.1.call-update
  10.1 0.0 reduce-scatter.3.cloned.1.call-start
  11.5 1.1 multiply_reduce_fusion.4
  12.6 1.1 multiply_convert_fusion.1
  13.6 9.8 all_gather.6
  23.4 144.5 %all-gather.2.cloned.1.call-done = bf16[4096,1152]{1,0:T(8,128)(2,1)} async-done(((bf16[64,1152]{1,0:T(8,128)(2,1)}), bf16[4096,1152]{1,0:T(8,128)(2,1)}) %all-gather.2.cloned.1.call-update) | async-done | bytes 9437200 | tf_op jit(solution)/shard_map/all_gather | solution.py:55
  167.9 10.9 fusion.14
  178.8 2.0 copy-done.3
  180.8 4.6 convolution_multiply_fusion.1
  185.4 0.0 reduce-scatter.3.cloned.1.call-update
  185.4 0.0 reduce-scatter.5.cloned.1.call-start
  185.5 12.9 %convolution_multiply_fusion = f32[4096,1152]{1,0:T(8,128)} fusion(bf16[256,1152]{1,0:T(8,128)(2,1)S(1)} %all_gather.6, f32[]{:T(128)} %bitcast, f32[256,4096]{1,0:T(8,128)} %copy-done.3, f32[]{:T(128)} %bitcast.11, s32[4096]{0:T(1024)S(1)} %fusion.12, s32[256]{0:T(256)S(1)} %iota_add_fusion), kind=kOutput, calls=%fused_computation | convolution fusion | flops 2432172032 | bytes 23675912 | tf_op jit(solution)/shard_map/dot_general | solution.py:31
  198.4 0.0 reduce-scatter.5.cloned.1.call-update
  198.4 76.4 %all-reduce = (f32[]{:T(128)}, f32[]{:T(128)}, f32[]{:T(128)}) all-reduce(f32[]{:T(128)} %get-tuple-element.7, f32[]{:T(128)} %get-tuple-element.6, f32[]{:T(128)} %get-tuple-element.5), channel_id=1, replica_groups=mesh['wide'=64,'narrow'=4] {'wide','narrow'}, use_global_device_ids=true, to_apply=%region_3.4 | all-reduce | flops 3 | bytes 24 | tf_op jit(solution)/shard_map/psum | solution.py:64
  276.8 0.0 reduce-scatter.3.cloned.1.call-done
  276.8 1.2 multiply_reduce_fusion.2
  278.0 1.8 subtract_multiply_fusion.1
  279.8 797.5 %reduce-scatter.5.cloned.1.call-done = f32[64,1152]{1,0:T(8,128)} async-done(((f32[4096,1152]{1,0:T(8,128)}), f32[64,1152]{1,0:T(8,128)}) %reduce-scatter.5.cloned.1.call-update) | async-done | bytes 294928 | tf_op jit(solution)/shard_map/reduce_scatter | solution.py:63
  1077.3 0.0 copy-done.1
  1077.3 1.2 multiply_reduce_fusion.1
  1078.5 1.8 subtract_multiply_fusion
  (10 shorter events, 0.0 us)
Async XLA Ops:
  7.2 160.7 %all-gather.2.cloned.1.call-start = ((), (), s32[]{:S(2)}) async-start(), calls=%async_computation.2 | async-start | bytes 9584640 | tf_op jit(solution)/shard_map/all_gather | solution.py:55
  10.1 266.7 %reduce-scatter.3.cloned.1.call-start = ((), (), s32[]{:S(2)}) async-start(), calls=%async_computation.3 | async-start | bytes 1474560 | tf_op jit(solution)/shard_map/reduce_scatter | solution.py:62
  167.9 12.9 %copy-start.2 = (bf16[4096,1152]{1,0:T(8,128)(2,1)S(1)}, bf16[4096,1152]{1,0:T(8,128)(2,1)}, u32[]{:S(2)}) copy-start(bf16[4096,1152]{1,0:T(8,128)(2,1)} %all-gather.2.cloned.1.call-done) | copy-start | bytes 28311556
  178.7 2.0 copy-start.3
  185.4 891.9 %reduce-scatter.5.cloned.1.call-start = ((), (), s32[]{:S(2)}) async-start(), calls=%async_computation.4 | async-start | bytes 19169280 | tf_op jit(solution)/shard_map/reduce_scatter | solution.py:63
  198.4 78.4 %copy-start = (f32[64,1152]{1,0:T(8,128)S(1)}, f32[64,1152]{1,0:T(8,128)}, u32[]{:S(2)}) copy-start(f32[64,1152]{1,0:T(8,128)} %param.4) | copy-start | bytes 884740
  198.4 879.0 %copy-start.1 = (f32[64,1152]{1,0:T(8,128)S(1)}, f32[64,1152]{1,0:T(8,128)}, u32[]{:S(2)}) copy-start(f32[64,1152]{1,0:T(8,128)} %param.5) | copy-start | bytes 884740
Sparse Core Ops, SparseCore 0:
  12.2 155.5 all-gather.1
  185.5 21.4 reduce-scatter.2
  213.2 864.0 reduce-scatter.4
where the time goes:
time: 1090 us
  waiting for transfers between devices  942 us (86%)
  blocking collectives  86.2 us (8%)
  matrix products  28.4 us (3%)
  between operations  20.5 us (2%)
  other arithmetic  10.9 us (1%)
    reduce_scatter x1, waiting for transfers between devices, on_device(): lax.psum_scatter(text_term, 'wide', scatter_dimension=0, tiled=True)  798 us
    all_gather x1, waiting for transfers between devices, on_device(): text_all = lax.all_gather(text_low, 'wide', axis=0, tiled=True)  144 us
    psum x1, blocking collectives, on_device(): lax.psum((loss_sum, temp_sum, bias_sum), ('wide', 'narrow'))  76.4 us
  transfers between devices with their start and end apart: 3, of which 2 were waited for; matrix products, arithmetic and copies ran while one was open for 2% of the time, Pallas kernels for 0%

commit v1 on v0

v1 whole, which is shorter than its diff:
```python
import jax
import jax.numpy as jnp
from jax import lax
from jax.sharding import Mesh
from jax.sharding import PartitionSpec as P

EPS = 1e-06
AXES = ("x", "yh", "z", "yl", "core")
PLANE = ("x", "yh", "yl")
COLUMN = ("z", "core")


def unit_rows(values):
    inverse = lax.rsqrt(jnp.sum(values * values, axis=1, keepdims=True) + EPS)
    return (values * inverse, inverse)


def back_rows(unit, inverse, direction):
    along = jnp.sum(unit * direction, axis=1, keepdims=True)
    return inverse * (direction - unit * along)


def pair_tile(rows_low, row_ids, text_all, text_ids, scale, offset):
    sim = lax.dot_general(
        rows_low, text_all, (((1,), (1,)), ((), ())), preferred_element_type=jnp.float32
    )
    logits = scale * sim + offset
    label = jnp.where(row_ids[:, None] == text_ids[None, :], 1.0, -1.0).astype(jnp.float32)
    loss_sum = jnp.sum(jax.nn.softplus(-label * logits))
    pair_grad = -label * jax.nn.sigmoid(-label * logits)
    temp_sum = jnp.sum(pair_grad * scale * sim)
    bias_sum = jnp.sum(pair_grad)
    pair_low = pair_grad.astype(jnp.bfloat16)
    image_dir = scale * jnp.dot(pair_low, text_all, preferred_element_type=jnp.float32)
    text_term = scale * lax.dot_general(
        pair_low, rows_low, (((0,), (0,)), ((), ())), preferred_element_type=jnp.float32
    )
    return (image_dir, text_term, loss_sum, temp_sum, bias_sum)


def on_device(image_embed, text_embed, log_temp, bias):
    rows = image_embed.shape[0]
    total = rows * 256
    image_unit, inv_image = unit_rows(image_embed)
    text_unit, inv_text = unit_rows(text_embed)
    image_low = image_unit.astype(jnp.bfloat16)
    text_low = text_unit.astype(jnp.bfloat16)
    scale = jnp.exp(log_temp[0])
    offset = bias[0]
    me = lax.axis_index(AXES)
    ids = me * rows + jnp.arange(rows, dtype=jnp.int32)
    text_all = lax.all_gather(text_low, PLANE, axis=0, tiled=True)
    image_all = lax.all_gather(image_low, COLUMN, axis=0, tiled=True)
    x, yh, z, yl, core = (lax.axis_index(a) for a in AXES)
    k = jnp.arange(16 * rows, dtype=jnp.int32)
    blk, off = k // rows, k % rows
    row_ids = ((((x * 2 + yh) * 8 + blk // 2) * 2 + yl) * 2 + blk % 2) * rows + off
    text_ids = (((blk // 2 * 8 + z) * 2 + blk % 2) * 2 + core) * rows + off
    image_dir, text_term, loss_sum, temp_sum, bias_sum = pair_tile(
        image_all, row_ids, text_all, text_ids, scale, offset
    )
    image_dir = lax.psum_scatter(image_dir, COLUMN, scatter_dimension=0, tiled=True)
    text_dir = lax.psum_scatter(text_term, PLANE, scatter_dimension=0, tiled=True)
    sums = lax.psum(jnp.stack([loss_sum, temp_sum, bias_sum]), AXES)
    image_grad = back_rows(image_unit, inv_image, image_dir)
    text_grad = back_rows(text_unit, inv_text, text_dir)
    sums = sums / total
    return (sums[0:1], image_grad, text_grad, sums[1:2], sums[2:3])


def solution(mesh):
    grid = Mesh(mesh.devices.reshape(4, 2, 8, 2, 2), AXES)
    rows = P(AXES, None)
    return jax.shard_map(
        on_device,
        mesh=grid,
        in_specs=(rows, rows, P(), P()),
        out_specs=(P(), rows, rows, P(), P()),
        check_vma=False,
    )
```

time: 1090 us -> 280 us (0.26)
  waiting for transfers between devices: 942 us -> 147 us
    reduce_scatter x2, waiting for transfers between devices: 798 us -> 53.3 us  [the longest x1 53.3 us: on_device(): lax.psum_scatter(image_dir, COLUMN, scatter_dimension=0, tiled=True)]
    all_gather x1 -> x2, waiting for transfers between devices: 144 us -> 93.4 us  [the longest x1 50.3 us: on_device(): text_all = lax.all_gather(text_low, PLANE, axis=0, tiled=True)]
  transfers between devices with their start and end apart: 3 -> 4, of which waited for: 2 -> 3; matrix products, arithmetic and copies ran while one was open for 2% -> 5% of each run, Pallas kernels for 0% -> 0%
where the time goes in v1:
time: 280 us; the launch traced here: 277 us
  waiting for transfers between devices  147 us (52%)
  blocking collectives  77.1 us (28%)
  matrix products  21 us (8%)
  between operations  15.2 us (5%)
  other arithmetic  13.7 us (5%)
  local copies, waits for them, and re-layouts  3.51 us (1%)
    psum x1, blocking collectives, on_device(): sums = lax.psum(jnp.stack([loss_sum, temp_sum, bias_sum]), AXES)  77.1 us
    reduce_scatter x1, waiting for transfers between devices, on_device(): lax.psum_scatter(image_dir, COLUMN, scatter_dimension=0, tiled=True)  53.3 us
    all_gather x1, waiting for transfers between devices, on_device(): text_all = lax.all_gather(text_low, PLANE, axis=0, tiled=True)  50.3 us
    all_gather x1, waiting for transfers between devices, on_device(): image_all = lax.all_gather(image_low, COLUMN, axis=0, tiled=True)  43.1 us
    dot_general x1, matrix products, pair_tile(): lax.dot_general(rows_low, text_all, (((1,), (1,)), ((), ())), preferred_e...  9.74 us
    dot_general x1, matrix products, pair_tile(): jnp.dot(pair_low, text_all, preferred_element_type=jnp.float32)  6.66 us
  transfers between devices with their start and end apart: 4, of which 3 were waited for; matrix products, arithmetic and copies ran while one was open for 5% of the time, Pallas kernels for 0%

profile of v1, /device:TPU:1, one launch (start us, length us, event | category | flops | bytes accessed | tf_op | source)
XLA Modules:
  0.0 277.4 jit_solution(5511018288432809470)
XLA Ops:
  7.2 0.0 all-gather.5.cloned.1.call-start
  7.2 1.1 multiply_reduce_fusion.3
  8.3 1.7 multiply_convert_fusion
  10.0 0.0 all-gather.5.cloned.1.call-update
  10.1 0.0 all-gather.3.cloned.1.call-start
  10.1 1.1 multiply_reduce_fusion.4
  11.2 1.7 multiply_convert_fusion.1
  12.9 0.0 reduce-scatter.5.cloned.1.call-start
  14.4 50.3 %all-gather.5.cloned.1.call-done = bf16[1024,1152]{1,0:T(8,128)(2,1)} async-done(((bf16[64,1152]{1,0:T(8,128)(2,1)}), bf16[1024,1152]{1,0:T(8,128)(2,1)}) %all-gather.5.cloned.1.call-update) | async-done | bytes 2359312 | tf_op jit(solution)/shard_map/all_gather | solution.py:52
  64.7 43.1 %all-gather.3.cloned.1.call-done = bf16[1024,1152]{1,0:T(8,128)(2,1)} async-done(((bf16[64,1152]{1,0:T(8,128)(2,1)}), bf16[1024,1152]{1,0:T(8,128)(2,1)}) %all-gather.3.cloned.1.call-update) | async-done | bytes 2359312 | tf_op jit(solution)/shard_map/all_gather | solution.py:53
  107.8 9.7 %fusion = (f32[]{:T(128)}, f32[]{:T(128)}, f32[]{:T(128)}, bf16[1024,1024]{1,0:T(8,128)(2,1)S(1)}) fusion(f32[]{:T(128)} %bitcast.11, f32[]{:T(128)} %bitcast, s32[1024]{0:T(1024)S(1)} %get-tuple-element.12, s32[1024]{0:T(1024)S(1)} %get-tuple-element.13, bf16[1024,1152]{1,0:T(8,128)(2,1)} %all-gather.3.cloned.1.call-done, ...), kind=kOutput, calls=%fused_computation.3 | convolution fusion | flops 2438987776 | bytes 6823956 | tf_op jit(solution)/shard_map/dot_general | solution.py:24
  117.5 1.3 copy-done.4
  118.8 4.6 %convolution_multiply_fusion = f32[1024,1152]{1,0:T(8,128)} fusion(bf16[1024,1152]{1,0:T(8,128)(2,1)S(1)} %copy-done.3, f32[]{:T(128)} %bitcast, bf16[1024,1024]{1,0:T(8,128)(2,1)S(1)} %get-tuple-element.8), kind=kOutput, calls=%fused_computation.1 | convolution fusion | flops 2417098752 | bytes 9175044 | tf_op jit(solution)/shard_map/dot_general | solution.py:35
  123.5 0.0 reduce-scatter.3.cloned.1.call-start
  123.5 1.6 copy-done.2
  125.1 6.7 %convolution_multiply_fusion.1 = f32[1024,1152]{1,0:T(8,128)} fusion(bf16[1024,1152]{1,0:T(8,128)(2,1)S(1)} %copy-done.2, f32[]{:T(128)} %bitcast, bf16[1024,1024]{1,0:T(8,128)(2,1)} %copy-done.4), kind=kOutput, calls=%fused_computation.2 | convolution fusion | flops 2417098752 | bytes 9175044 | tf_op jit(solution)/shard_map/dot_general | solution.py:34
  131.8 2.1 pad_maximum_fusion
  133.9 77.1 %psum.7 = f32[3]{0:T(128)S(1)} all-reduce(f32[3]{0:T(128)S(1)} %pad_maximum_fusion), channel_id=1, replica_groups=mesh['x'=4,'yh'=2,'z'=8,'yl'=2,'core'=2] {'x','yh','z','yl','core'}, use_global_device_ids=true, to_apply=%region_5.6 | all-reduce | flops 3 | bytes 24 | tf_op jit(solution)/shard_map/psum | solution.py:64
  211.0 0.6 fusion.17
  211.6 1.2 multiply_reduce_fusion.1
  212.8 1.8 subtract_multiply_fusion
  214.6 53.3 %reduce-scatter.3.cloned.1.call-done = f32[64,1152]{1,0:T(8,128)} async-done(((f32[1024,1152]{1,0:T(8,128)}), f32[64,1152]{1,0:T(8,128)}) %reduce-scatter.3.cloned.1.call-update) | async-done | bytes 294928 | tf_op jit(solution)/shard_map/reduce_scatter | solution.py:62
  267.9 1.2 multiply_reduce_fusion.2
  269.1 1.8 subtract_multiply_fusion.1
  (16 shorter events, 0.1 us)
Async XLA Ops:
  7.2 57.5 %all-gather.5.cloned.1.call-start = ((), (), s32[]{:S(2)}) async-start(), calls=%async_computation.3 | async-start | bytes 2506752 | tf_op jit(solution)/shard_map/all_gather | solution.py:52
  10.1 97.7 %all-gather.3.cloned.1.call-start = ((), (), s32[]{:S(2)}) async-start(), calls=%async_computation.2 | async-start | bytes 2506752 | tf_op jit(solution)/shard_map/all_gather | solution.py:53
  12.9 198.7 %reduce-scatter.5.cloned.1.call-start = ((), (), s32[]{:S(2)}) async-start(), calls=%async_computation.5 | async-start | bytes 5013504 | tf_op jit(solution)/shard_map/reduce_scatter | solution.py:63
  107.8 11.1 %copy-start.3 = (bf16[1024,1152]{1,0:T(8,128)(2,1)S(1)}, bf16[1024,1152]{1,0:T(8,128)(2,1)}, u32[]{:S(2)}) copy-start(bf16[1024,1152]{1,0:T(8,128)(2,1)} %all-gather.3.cloned.1.call-done) | copy-start | bytes 7077892
  117.5 1.3 copy-start.4
  123.4 1.7 copy-start.2
  123.5 144.5 %reduce-scatter.3.cloned.1.call-start = ((), (), s32[]{:S(2)}) async-start(), calls=%async_computation.4 | async-start | bytes 5013504 | tf_op jit(solution)/shard_map/reduce_scatter | solution.py:62
  131.8 79.9 %copy-start = (f32[64,1152]{1,0:T(8,128)S(1)}, f32[64,1152]{1,0:T(8,128)}, u32[]{:S(2)}) copy-start(f32[64,1152]{1,0:T(8,128)} %param.5) | copy-start | bytes 884740
  131.8 136.2 %copy-start.1 = (f32[64,1152]{1,0:T(8,128)S(1)}, f32[64,1152]{1,0:T(8,128)}, u32[]{:S(2)}) copy-start(f32[64,1152]{1,0:T(8,128)} %param.4) | copy-start | bytes 884740
Sparse Core Ops, SparseCore 0:
  11.1 53.5 all-gather.4
  67.1 40.6 all-gather.2
  123.6 80.0 reduce-scatter.4
  206.1 61.7 reduce-scatter.2

commit v2 on v1

v2 whole, which is shorter than its diff:
```python
import math

import jax
import jax.numpy as jnp
from jax import lax
from jax.experimental import pallas as pl
from jax.experimental.pallas import tpu as pltpu
from jax.sharding import Mesh
from jax.sharding import PartitionSpec as P

EPS = 1e-06
LOG2E = 1.0 / math.log(2.0)
LN2 = math.log(2.0)
AXES = ("x", "yh", "z", "yl", "core")
NX, NY, NZ = 4, 4, 8
ROWS, D = 64, 1152
HALF = ROWS // 2
SIDE = 16 * ROWS
TOTAL = 256 * ROWS
f32, bf16 = jnp.float32, jnp.bfloat16
NSEM = 128


def place():
    x, yh, z, yl, core = (lax.axis_index(a) for a in AXES)
    return x, yh * 2 + yl, z, core


def peer(dx=0, dy=0, dz=0, dc=0):
    x, y, z, core = place()
    y = lax.rem(y + dy, NY)
    return (
        lax.rem(x + dx, NX),
        y // 2,
        lax.rem(z + dz, NZ),
        lax.rem(y, 2),
        lax.rem(core + dc, 2),
    )


PEERS = (
    [dict(dx=d) for d in (1, 2, 3)]
    + [dict(dy=d) for d in (1, 2, 3)]
    + [dict(dz=d) for d in range(1, NZ)]
    + [dict(dc=1)]
)


def fold(v):
    r, c = v.shape
    v = v.reshape(r // 8, 8, c).sum(0)
    return sum(v[:, k * 128 : (k + 1) * 128] for k in range(c // 128))


def pair_terms(sim, scale2, offset2):
    t2 = sim * scale2
    l2 = t2 + offset2
    e = jnp.exp2(l2)
    r = 1.0 / (1.0 + e)
    p = e * r
    small = e * (1.0 - e * (0.5 - e * (1.0 / 3.0 - e * 0.25)))
    sp = jnp.where(e < 0.01, small, jnp.log(1.0 + e))
    return t2, l2, p, r, sp


def dot_nt(a, b):
    return lax.dot_general(a, b, (((1,), (1,)), ((), ())), preferred_element_type=f32)


def dot_tn(a, b):
    return lax.dot_general(a, b, (((0,), (0,)), ((), ())), preferred_element_type=f32)


def rows_at(slot, half=None, count=1):
    if half is None:
        return pl.ds(slot * ROWS, count * ROWS)
    return pl.ds(slot * ROWS + half * HALF, HALF)


def kernel(
    logt_ref, bias_ref, img_ref, txt_ref,
    gimg_ref, gtxt_ref, sums_ref,
    I, T, pair, PI, PT, PTb, SI, XA, YB, QA, QB, RA, RB, ZL, ZR, acc, S,
    ssem, rsem,
):
    barrier = pltpu.get_barrier_semaphore()
    for p in PEERS:
        pl.semaphore_signal(barrier, 1, device_id=peer(**p), device_id_type=pl.DeviceIdType.MESH)

    used = [0]

    def send(src, dst, **to):
        k = used[0]
        used[0] += 1
        c = pltpu.make_async_remote_copy(
            src_ref=src, dst_ref=dst, send_sem=ssem.at[k], recv_sem=rsem.at[k],
            device_id=peer(**to), device_id_type=pl.DeviceIdType.MESH,
        )
        c.start()
        sent.append(c)
        return c

    sent = []

    def inverse(ref):
        v = ref[...]
        return lax.rsqrt(jnp.sum(v * v, axis=1, keepdims=True) + EPS)

    inv_img = inverse(img_ref)
    inv_txt = inverse(txt_ref)
    I[rows_at(0), :] = (img_ref[...] * inv_img).astype(bf16)
    T[rows_at(0), :] = (txt_ref[...] * inv_txt).astype(bf16)
    scale = jnp.exp(jnp.full((8, 128), logt_ref[0], f32))[0:1, 0:1]
    scale2 = scale * LOG2E
    offset2 = jnp.full((1, 1), bias_ref[0] * LOG2E, f32)
    acc[...] = jnp.zeros_like(acc)
    pl.semaphore_wait(barrier, len(PEERS))

    right, left, plane1 = {}, {}, {}
    sib = []

    def ring(step):
        for h in (0, 1):
            if step < 4 or h == 0:
                if step > 1:
                    right[step - 1, h].wait_recv()
                right[step, h] = send(I.at[rows_at(step - 1, h)], I.at[rows_at(step, h)], dz=1)
            if step < 4 or h == 1:
                if step > 1:
                    left[step - 1, h].wait_recv()
                src = (9 - step) % 8
                left[step, h] = send(I.at[rows_at(src, h)], I.at[rows_at(8 - step, h)], dz=7)

    def to_sibling(slot):
        sib.append(send(I.at[rows_at(slot)], I.at[rows_at(8 + slot)], dc=1))

    for d in (1, 3, 2):
        plane1[d, 0] = send(T.at[rows_at(0, 0)], T.at[rows_at(d * 4, 0)], dx=d)
        plane1[d, 1] = send(T.at[rows_at(0, 1)], T.at[rows_at(d, 1)], dy=d)
    ring(1)
    to_sibling(0)
    plane2 = []

    def forward(e):
        for f in (1, 3, 2):
            plane2.append(send(T.at[rows_at(e * 4, 0)], T.at[rows_at(e * 4 + f, 0)], dy=f))
            plane2.append(send(T.at[rows_at(e, 1)], T.at[rows_at(f * 4 + e, 1)], dx=f))

    forward(0)
    ring(2)
    for d in (1, 3, 2):
        plane1[d, 0].wait_recv()
        plane1[d, 1].wait_recv()
        forward(d)
    to_sibling(1)
    to_sibling(7)
    ring(3)
    to_sibling(2)
    to_sibling(6)
    ring(4)
    right[3, 1].wait_recv()
    left[3, 0].wait_recv()
    to_sibling(3)
    to_sibling(5)
    right[4, 0].wait_recv()
    left[4, 1].wait_recv()
    to_sibling(4)
    for c in plane2:
        c.wait_recv()
    for c in sib:
        c.wait_recv()

    CH, RBK = 256, 256

    @pl.loop(0, SIDE // CH)
    def _(j):
        js = pl.ds(pl.multiple_of(j * CH, CH), CH)
        tj = T[js, :]
        for r in range(SIDE // RBK):
            rs = slice(r * RBK, (r + 1) * RBK)
            t2, _, p, _, sp = pair_terms(dot_nt(I[rs, :], tj), scale2, offset2)
            pair[rs, js] = p.astype(bf16)
            acc[0] += fold(sp)
            acc[1] += fold(p)
            acc[2] += fold(p * t2)

    t2, l2, p, r, _ = pair_terms(dot_nt(I[0:ROWS, :], T[0 : 2 * ROWS, :]), scale2, offset2)
    shape = (ROWS, 2 * ROWS)
    same = lax.broadcasted_iota(jnp.int32, shape, 0) == lax.broadcasted_iota(jnp.int32, shape, 1)
    pair[0:ROWS, 0 : 2 * ROWS] = jnp.where(same, -r, p).astype(bf16)
    acc[0] -= fold(jnp.where(same, l2 * LN2, 0.0))
    acc[1] -= fold(jnp.where(same, 1.0, 0.0))
    acc[2] -= fold(jnp.where(same, t2, 0.0))

    mine = place()
    sizes = (NX, NY, NZ, 2)
    names = ("dx", "dy", "dz", "dc")
    stage_copies = {}

    def sums_start(stage, value):
        at = S.at[stage, mine[stage]]
        S[stage, mine[stage]] = value
        stage_copies[stage] = [
            send(at, at, **{names[stage]: d}) for d in range(1, sizes[stage])
        ]

    def sums_next(stage):
        for c in stage_copies[stage]:
            c.wait()
        value = S[stage, 0]
        for k in range(1, sizes[stage]):
            value = value + S[stage, k]
        return value

    row = lax.broadcasted_iota(jnp.int32, (8, 128), 0)
    lanes = [jnp.sum(acc[k], axis=0, keepdims=True) for k in range(3)]
    first = jnp.where(row == 0, lanes[0], jnp.where(row == 1, lanes[1], lanes[2]))
    sums_start(0, first)

    def image_part(base, count, block=256):
        @pl.loop(0, count // block)
        def _(i):
            rs = pl.ds(pl.multiple_of(base + i * block, block), block)
            PI[rs, :] = jnp.dot(pair[rs, :], T[...], preferred_element_type=f32)

    def text_part(dx):
        js = pl.ds(dx * 256, 256)
        v = dot_tn(pair[:, js], I[...])
        PT[js, :] = v
        PTb[js, :] = v.astype(bf16)

    xa, yb = {}, {}

    def plane_send(dx):
        for dy in range(4):
            slot = dx * 4 + dy
            if dx:
                xa[dx, dy] = send(PTb.at[rows_at(slot, 0)], XA.at[dx - 1, dy], dx=(NX - dx))
            if dy:
                yb[dx, dy] = send(PTb.at[rows_at(slot, 1)], YB.at[dy - 1, dx], dy=(NY - dy))

    image_part(512, 512)
    sib2 = [send(PI.at[rows_at(8 + 2 * k, count=2)], SI.at[rows_at(2 * k, count=2)], dc=1) for k in (2, 1, 3, 0)]
    sib2 = {2: sib2[0], 1: sib2[1], 3: sib2[2], 0: sib2[3]}
    text_part(2)
    plane_send(2)
    image_part(256, 256)
    zl, zr = {}, {}

    def chain(dirn, slot, h):
        rs = rows_at(slot, h)
        v = PI[rs, :] + SI[rs, :]
        got = (zl if dirn == "l" else zr).get((slot, h))
        if got is not None:
            got.wait_recv()
            v = v + (ZL if dirn == "l" else ZR)[rs, :]
        PI[rs, :] = v
        if dirn == "l":
            zl[slot - 1, h] = send(PI.at[rs], ZL.at[rows_at(slot - 1, h)], dz=NZ - 1)
        else:
            nxt = (slot + 1) % 8
            zr[nxt, h] = send(PI.at[rs], ZR.at[rows_at(nxt, h)], dz=1)

    sib2[2].wait_recv()
    chain("l", 4, 0)
    chain("r", 4, 1)
    chain("r", 5, 0)
    image_part(0, 256)
    sib2[1].wait_recv()
    chain("l", 3, 1)
    text_part(1)
    plane_send(1)
    sums_start(1, sums_next(0))
    text_part(3)
    plane_send(3)
    chain("l", 3, 0)
    chain("r", 5, 1)
    text_part(0)
    plane_send(0)
    sib2[3].wait_recv()
    chain("l", 2, 1)
    chain("r", 6, 0)
    sums_start(2, sums_next(1))
    chain("l", 2, 0)
    chain("r", 6, 1)
    sib2[0].wait_recv()

    ra, rb = {}, {}

    def second(k):
        va = PT[rows_at(k, 0), :]
        vb = PT[rows_at(k * 4, 1), :]
        for d in (1, 2, 3):
            xa[d, k].wait_recv()
            va = va + XA[d - 1, k].astype(f32)
            yb[k, d].wait_recv()
            vb = vb + YB[d - 1, k].astype(f32)
        QA[k] = va
        QB[k] = vb
        if k:
            ra[k] = send(QA.at[k], RA.at[k - 1], dy=NY - k)
            rb[k] = send(QB.at[k], RB.at[k - 1], dx=NX - k)

    second(2)
    chain("l", 1, 1)
    chain("r", 7, 0)
    second(1)
    sums_start(3, sums_next(2))
    chain("l", 1, 0)
    chain("r", 7, 1)
    second(3)
    second(0)

    total = sums_next(3)
    sums_ref[...] = jnp.broadcast_to(jnp.sum(total, axis=1, keepdims=True), (8, 128))

    def back(ref, inv, direction):
        unit = ref[...] * inv
        along = jnp.sum(unit * direction, axis=1, keepdims=True)
        return inv * (direction - unit * along)

    for k in (1, 3, 2):
        ra[k].wait_recv()
        rb[k].wait_recv()
        QA[0] = QA[0] + RA[k - 1]
        QB[0] = QB[0] + RB[k - 1]
    tdir = jnp.concatenate([QA[0], QB[0]], axis=0) * scale
    gtxt_ref[...] = back(txt_ref, inv_txt, tdir)
    for h in (0, 1):
        zl[0, h].wait_recv()
        zr[0, h].wait_recv()
    own = rows_at(0)
    idir = (PI[own, :] + SI[own, :] + ZL[own, :] + ZR[own, :]) * scale
    gimg_ref[...] = back(img_ref, inv_img, idir)

    done = set()
    for stage in stage_copies:
        done.update(id(c) for c in stage_copies[stage])
    for c in sent:
        if id(c) not in done:
            c.wait_send()


def on_device(image_embed, text_embed, log_temp, bias):
    vmem = pl.BlockSpec(memory_space=pltpu.VMEM)
    smem = pl.BlockSpec(memory_space=pltpu.SMEM)
    grad = jax.ShapeDtypeStruct((ROWS, D), f32)
    gimg, gtxt, sums = pl.pallas_call(
        kernel,
        out_shape=(grad, grad, jax.ShapeDtypeStruct((8, 128), f32)),
        in_specs=[smem, smem, vmem, vmem],
        out_specs=(vmem, vmem, vmem),
        scratch_shapes=[
            pltpu.VMEM((SIDE, D), bf16),
            pltpu.VMEM((SIDE, D), bf16),
            pltpu.VMEM((SIDE, SIDE), bf16),
            pltpu.VMEM((SIDE, D), f32),
            pltpu.VMEM((SIDE, D), f32),
            pltpu.VMEM((SIDE, D), bf16),
            pltpu.VMEM((8 * ROWS, D), f32),
            pltpu.VMEM((3, 4, HALF, D), bf16),
            pltpu.VMEM((3, 4, HALF, D), bf16),
            pltpu.VMEM((4, HALF, D), f32),
            pltpu.VMEM((4, HALF, D), f32),
            pltpu.VMEM((3, HALF, D), f32),
            pltpu.VMEM((3, HALF, D), f32),
            pltpu.VMEM((8 * ROWS, D), f32),
            pltpu.VMEM((8 * ROWS, D), f32),
            pltpu.VMEM((3, 8, 128), f32),
            pltpu.VMEM((4, 8, 8, 128), f32),
            pltpu.SemaphoreType.DMA((NSEM,)),
            pltpu.SemaphoreType.DMA((NSEM,)),
        ],
        compiler_params=pltpu.CompilerParams(
            collective_id=0, has_side_effects=True, vmem_limit_bytes=56 * 2**20
        ),
    )(log_temp, bias, image_embed, text_embed)
    loss = sums[0, 0:1] / TOTAL
    bias_grad = sums[1, 0:1] / TOTAL
    temp_grad = sums[2, 0:1] * (LN2 / TOTAL)
    return (loss, gimg, gtxt, temp_grad, bias_grad)


def solution(mesh):
    grid = Mesh(mesh.devices.reshape(NX, NY // 2, NZ, 2, 2), AXES)
    rows = P(AXES, None)
    return jax.shard_map(
        on_device,
        mesh=grid,
        in_specs=(rows, rows, P(), P()),
        out_specs=(P(), rows, rows, P(), P()),
        check_vma=False,
    )
```

time: 280 us -> 78.4 us (0.28)
  waiting for transfers between devices: 147 us -> 0 us
  blocking collectives: 77.1 us -> 0 us
  Pallas kernels: 0 us -> 67.1 us
  matrix products: 21 us -> 0 us
  other arithmetic: 13.7 us -> 0 us
  between operations: 15.2 us -> 7.28 us
    all_gather x2 -> x0, waiting for transfers between devices: 93.4 us -> none  [the longest x1 50.3 us: on_device(): text_all = lax.all_gather(text_low, PLANE, axis=0, tiled=True)]
    psum x1 -> x0, blocking collectives: 77.1 us -> none  [on_device(): sums = lax.psum(jnp.stack([loss_sum, temp_sum, bias_sum]), AXES)]
    pallas_call x0 -> x1, Pallas kernels: none -> 67.1 us  [on_device(): pl.pallas_call(kernel, out_shape=(grad, grad, jax.ShapeDtypeStruct((8, 12...]
    reduce_scatter x2 -> x0, waiting for transfers between devices: 53.3 us -> none  [the longest x1 53.3 us: on_device(): lax.psum_scatter(image_dir, COLUMN, scatter_dimension=0, tiled=True)]
    dot_general x3 -> x0, matrix products: 21 us -> none  [the longest x1 9.74 us: pair_tile(): lax.dot_general(rows_low, text_all, (((1,), (1,)), ((), ())), preferred_e...]
    reduce_sum x4 -> x0, other arithmetic: 4.51 us -> none  [the longest x2 2.35 us: back_rows(): along = jnp.sum(unit * direction, axis=1, keepdims=True)]
    mul x2 -> x0, other arithmetic: 3.6 us -> none  [back_rows(): return inverse * (direction - unit * along)]
    convert_element_type x2 -> x0, other arithmetic: 3.44 us -> none  [the longest x1 1.72 us: on_device(): image_low = image_unit.astype(jnp.bfloat16)]
  transfers between devices with their start and end apart: 4 -> 0, of which waited for: 3 -> 0; matrix products, arithmetic and copies ran while one was open for 5% -> 0% of each run, Pallas kernels for 0% -> 0%
where the time goes in v2:
time: 78.4 us; the launch traced here: 78.2 us
  Pallas kernels  67.1 us (86%)
  between operations  7.28 us (9%)
  local copies, waits for them, and re-layouts  3.76 us (5%)
    pallas_call x1, Pallas kernels, on_device(): pl.pallas_call(kernel, out_shape=(grad, grad, jax.ShapeDtypeStruct((8, 12...  67.1 us
    unnamed x4, local copies, waits for them, and re-layouts  2.46 us

profile of v2, /device:TPU:1, one launch (start us, length us, event | category | flops | bytes accessed | tf_op | source)
XLA Modules:
  0.0 78.2 jit_solution(17684600314140221432)
XLA Ops:
  1.9 67.1 %shard_map.83 = (f32[64,1152]{1,0:T(8,128)}, f32[64,1152]{1,0:T(8,128)}, f32[8,128]{1,0:T(8,128)}) custom-call(f32[1]{0:T(128)S(6)} %copy.11.logt_ref, f32[1]{0:T(128)S(6)} %copy.12.bias_ref, f32[64,1152]{1,0:T(8,128)} %img_ref.1, f32[64,1152]{1,0:T(8,128)} %txt_ref.1), custom_call_target="tpu_custom_call" | custom-call | tf_op jit(solution)/shard_map/pallas_call | solution.py:348
  69.0 1.3 %fusion = (f32[1,1]{1,0:T(1,128)}, f32[1,1]{1,0:T(1,128)}, f32[1,1]{1,0:T(1,128)}) fusion(f32[8,128]{1,0:T(8,128)} %get-tuple-element.8), kind=kLoop, calls=%fused_computation | loop fusion | bytes 24 | tf_op jit(solution)/shard_map/slice | solution.py:379
  72.3 0.0 copy-start
  72.3 1.7 %copy.13 = f32[64,1152]{1,0:T(8,128)} copy(f32[64,1152]{1,0:T(8,128)} %get-tuple-element.20) | data formatting | bytes 589824
  74.0 0.0 copy-done
  74.0 0.7 copy.14
Async XLA Ops:
  72.3 1.8 %copy-start = (f32[64,1152]{1,0:T(8,128)S(1)}, f32[64,1152]{1,0:T(8,128)}, u32[]{:S(2)}) copy-start(f32[64,1152]{1,0:T(8,128)} %get-tuple-element.21) | copy-start | bytes 884740

commit v3 on v1

v3 whole, which is shorter than its diff:
```python
import math

import jax
import jax.numpy as jnp
from jax import lax
from jax.experimental import pallas as pl
from jax.experimental.pallas import tpu as pltpu
from jax.sharding import Mesh
from jax.sharding import PartitionSpec as P

EPS = 1e-06
LOG2E = 1.0 / math.log(2.0)
LN2 = math.log(2.0)
AXES = ("x", "yh", "z", "yl", "core")
NX, NY, NZ = 4, 4, 8
ROWS, D = 64, 1152
HALF = ROWS // 2
QROWS = ROWS // 4
SIDE = 16 * ROWS
QUAD = 4 * ROWS
TOTAL = 256 * ROWS
NARROW_HOPS = 2
NSEM = 160
f32, bf16 = jnp.float32, jnp.bfloat16

IMAGE_AT = {4: 0, 3: 1, 5: 2, 2: 3, 6: 4, 1: 5, 7: 6, 0: 7}
CHUNK_AT = {0: 0, 1: 1, 3: 2, 2: 3}

PEERS = (
    [dict(dx=d) for d in (1, 2, 3)]
    + [dict(dy=d) for d in (1, 2, 3)]
    + [dict(dz=d) for d in range(1, NZ)]
    + [dict(dc=1)]
)


def place():
    x, yh, z, yl, core = (lax.axis_index(a) for a in AXES)
    return x, yh * 2 + yl, z, core


def peer(dx=0, dy=0, dz=0, dc=0):
    x, y, z, core = place()
    y = lax.rem(y + dy, NY)
    return (
        lax.rem(x + dx, NX),
        y // 2,
        lax.rem(z + dz, NZ),
        lax.rem(y, 2),
        lax.rem(core + dc, 2),
    )


def fold(v):
    r, c = v.shape
    v = v.reshape(r // 8, 8, c).sum(0)
    return sum(v[:, k * 128 : (k + 1) * 128] for k in range(c // 128))


def pair_terms(sim, scale2, offset2):
    t2 = sim * scale2
    l2 = t2 + offset2
    e = jnp.exp2(l2)
    r = 1.0 / (1.0 + e)
    p = e * r
    small = e * (1.0 - e * (0.5 - e * (1.0 / 3.0 - e * 0.25)))
    sp = jnp.where(e < 0.01, small, jnp.log(1.0 + e))
    return t2, l2, p, r, sp


def dot_nt(a, b):
    return lax.dot_general(a, b, (((1,), (1,)), ((), ())), preferred_element_type=f32)


def dot_tn(a, b):
    return lax.dot_general(a, b, (((0,), (0,)), ((), ())), preferred_element_type=f32)


def img(slot, half=None, other=0):
    start = other * 8 * ROWS + IMAGE_AT[slot] * ROWS
    if half is None:
        return pl.ds(start, ROWS)
    return pl.ds(start + half * HALF, HALF)


def ta(dx, dy):
    return pl.ds(CHUNK_AT[dx] * QUAD + dy * HALF, HALF)


def tb(dx, dy):
    return pl.ds(CHUNK_AT[dy] * QUAD + QUAD // 2 + dx * HALF, HALF)


def kernel(
    logt_hbm, bias_hbm, img_ref, txt_ref,
    dimg_ref, dtxt_ref, sums_ref,
    logt_ref, bias_ref, I, T, pair, PI, PIb, PT, PTb, SI,
    XA, XB, QA, QB, RA, RB, ZL, ZR, ZLb, ZRb, acc, S,
    lsem, ssem, rsem,
):
    barrier = pltpu.get_barrier_semaphore()
    for p in PEERS:
        pl.semaphore_signal(barrier, 1, device_id=peer(**p), device_id_type=pl.DeviceIdType.MESH)
    fetch = [
        pltpu.make_async_copy(src, dst, lsem.at[k])
        for k, (src, dst) in enumerate(
            ((logt_hbm, logt_ref), (bias_hbm, bias_ref))
        )
    ]
    for c in fetch:
        c.start()

    sent = []

    def send(src, dst, **to):
        k = len(sent)
        c = pltpu.make_async_remote_copy(
            src_ref=src, dst_ref=dst, send_sem=ssem.at[k], recv_sem=rsem.at[k],
            device_id=peer(**to), device_id_type=pl.DeviceIdType.MESH,
        )
        c.start()
        sent.append(c)
        return c

    def unit_low(ref):
        v = ref[...]
        return (v * lax.rsqrt(jnp.sum(v * v, axis=1, keepdims=True) + EPS)).astype(bf16)

    low = unit_low(txt_ref)
    T[ta(0, 0), :] = low[:HALF]
    T[tb(0, 0), :] = low[HALF:]
    I[img(0), :] = unit_low(img_ref)
    pl.semaphore_wait(barrier, len(PEERS))

    right, left, first, near, far, sib = {}, {}, {}, {}, {}, {}

    def quarter(slot, q):
        return pl.ds(IMAGE_AT[slot] * ROWS + q * QROWS, QROWS)

    def ring(step, *quarters):
        for q in quarters:
            if step < 4 or q < 2:
                if step > 1:
                    right[step - 1, q].wait_recv()
                right[step, q] = send(
                    I.at[quarter(step - 1, q)], I.at[quarter(step, q)], dz=1
                )
            if step < 4 or q >= 2:
                if step > 1:
                    left[step - 1, q].wait_recv()
                left[step, q] = send(
                    I.at[quarter((9 - step) % 8, q)], I.at[quarter(8 - step, q)], dz=NZ - 1
                )

    def to_sibling(slot):
        sib[slot] = send(I.at[img(slot)], I.at[img(slot, other=1)], dc=1)

    def forward(e):
        for f in (1, 3) if e != 2 else (2, 1, 3):
            near["a", e, f] = send(T.at[ta(e, 0)], T.at[ta(e, f)], dy=f)
            near["b", e, f] = send(T.at[tb(0, e)], T.at[tb(f, e)], dx=f)

    def forward_far(e):
        f = 1 if e == 0 else 3
        near["a", e, f].wait_recv()
        far["a", e] = send(T.at[ta(e, f)], T.at[ta(e, 2)], dy=f)
        near["b", e, f].wait_recv()
        far["b", e] = send(T.at[tb(f, e)], T.at[tb(2, e)], dx=f)

    def arrived(e):
        if e == 2:
            for f in (1, 3, 2):
                near["a", e, f].wait_recv()
                near["b", e, f].wait_recv()
            return
        f = 3 if e == 0 else 1
        near["a", e, f].wait_recv()
        near["b", e, f].wait_recv()
        far["a", e].wait_recv()
        far["b", e].wait_recv()

    def piece(q, e):
        rs = slice(q * QUAD, (q + 1) * QUAD)
        js = slice(CHUNK_AT[e] * QUAD, (CHUNK_AT[e] + 1) * QUAD)
        t2, _, p, _, sp = pair_terms(dot_nt(I[rs, :], T[js, :]), scale2, offset2)
        pair[rs, js] = p.astype(bf16)
        acc[0] += fold(sp)
        acc[1] += fold(p)
        acc[2] += fold(p * t2)

    def first_send(*ds):
        for d in ds:
            first["a", d] = send(T.at[ta(0, 0)], T.at[ta(d, 0)], dx=d)
            first["b", d] = send(T.at[tb(0, 0)], T.at[tb(0, d)], dy=d)

    def first_wait(d):
        first["a", d].wait_recv()
        first["b", d].wait_recv()

    first_send(1, 3)
    ring(1, 0, 1, 2, 3)
    forward(0)
    first_send(2)
    to_sibling(0)
    for c in fetch:
        c.wait()
    scale2 = jnp.exp(jnp.full((8, 128), logt_ref[0], f32))[0:1, 0:1] * LOG2E
    offset2 = jnp.full((1, 1), bias_ref[0] * LOG2E, f32)
    acc[...] = jnp.zeros_like(acc)
    ring(2, 0, 1)
    first_wait(1)
    forward(1)
    first_wait(3)
    forward(3)
    ring(2, 2, 3)
    to_sibling(1)
    to_sibling(7)
    ring(3, 0)
    forward_far(0)
    first_wait(2)
    forward(2)
    ring(3, 1, 2, 3)
    to_sibling(2)
    to_sibling(6)
    forward_far(1)
    ring(4, 0, 1)
    forward_far(3)
    ring(4, 2, 3)
    arrived(0)
    piece(1, 0)
    for q in (2, 3):
        right[3, q].wait_recv()
        left[3, q - 2].wait_recv()
    to_sibling(3)
    to_sibling(5)
    for k in (0, 1, 7, 2, 6):
        sib[k].wait_recv()
    piece(3, 0)
    for q in (0, 1):
        right[4, q].wait_recv()
        left[4, q + 2].wait_recv()
    to_sibling(4)
    arrived(1)
    piece(1, 1)
    piece(3, 1)
    piece(0, 0)
    piece(0, 1)
    arrived(3)
    piece(1, 3)
    piece(3, 3)
    piece(0, 3)
    arrived(2)
    piece(0, 2)
    piece(1, 2)
    piece(3, 2)
    for k in (3, 5, 4):
        sib[k].wait_recv()
    for e in (0, 1, 3, 2):
        piece(2, e)

    def image_part(q, n=4, first=0):
        start = q * QUAD + first * ROWS
        rs = slice(start, start + n * ROWS)
        PI[rs, :] = jnp.dot(pair[rs, :], T[...], preferred_element_type=f32)

    def text_part(e):
        js = slice(CHUNK_AT[e] * QUAD, (CHUNK_AT[e] + 1) * QUAD)
        v = dot_tn(pair[:, js], I[...])
        if e == 2:
            PTb[js, :] = v.astype(bf16)
        else:
            PT[js, :] = v

    part = {}

    def part_to_sibling(q, n=4, first=0):
        at = q * QUAD + first * ROWS
        part[q, first] = send(
            PI.at[pl.ds(2 * QUAD + at, n * ROWS)], SI.at[pl.ds(at, n * ROWS)], dc=1
        )

    zl, zr = {}, {}

    def chain(way, slot, h):
        hops, got, far_buf, low_buf = (
            (zl, zl.get((slot, h)), ZL, ZLb) if way == "l" else (zr, zr.get((slot, h)), ZR, ZRb)
        )
        rs = img(slot, h)
        v = PI[rs, :] + SI[rs, :]
        hop = 1
        if got is not None:
            copy, hop = got
            copy.wait_recv()
            v = v + (low_buf if hop <= NARROW_HOPS else far_buf)[rs, :].astype(f32)
            hop += 1
        nxt = slot - 1 if way == "l" else (slot + 1) % 8
        to = NZ - 1 if way == "l" else 1
        if hop <= NARROW_HOPS:
            PIb[rs, :] = v.astype(bf16)
            c = send(PIb.at[rs], low_buf.at[img(nxt, h)], dz=to)
        else:
            PI[rs, :] = v
            c = send(PI.at[rs], far_buf.at[img(nxt, h)], dz=to)
        hops[nxt, h] = (c, hop)

    xa, xb = {}, {}

    def plane_first():
        for k in (2, 3, 0, 1):
            way, at = (3, 1) if k % 2 == 0 else (1, 3)
            xa[at, k] = send(PTb.at[ta(2, k)], XA.at[at, k], dx=way)
            xb[at, k] = send(PTb.at[tb(k, 2)], XB.at[at, k], dy=way)

    def plane_next(e, late):
        way, at = (3, 0) if e == 1 else (1, 2)
        for k in (2, 3, 0, 1):
            if ((e, k) in xa) != late:
                continue
            va, vb = PT[ta(e, k), :], PT[tb(k, e), :]
            if late:
                xa[e, k].wait_recv()
                va = va + XA[e, k].astype(f32)
                xb[e, k].wait_recv()
                vb = vb + XB[e, k].astype(f32)
            PTb[ta(e, k), :] = va.astype(bf16)
            xa[at, k] = send(PTb.at[ta(e, k)], XA.at[at, k], dx=way)
            PTb[tb(k, e), :] = vb.astype(bf16)
            xb[at, k] = send(PTb.at[tb(k, e)], XB.at[at, k], dy=way)

    def plane_sum(k):
        for c in (xa[0, k], xa[2, k], xb[0, k], xb[2, k]):
            c.wait_recv()
        QA[k] = PT[ta(0, k), :] + XA[0, k].astype(f32) + XA[2, k].astype(f32)
        QB[k] = PT[tb(k, 0), :] + XB[0, k].astype(f32) + XB[2, k].astype(f32)

    lo, hi = pl.ds(0, HALF // 2), pl.ds(HALF // 2, HALF // 2)
    ra, rb = {}, {}

    def second_far():
        for at, rs, way in ((1, lo, 3), (3, hi, 1)):
            ra[at] = send(QA.at[2, rs], RA.at[at, rs], dy=way)
            rb[at] = send(QB.at[2, rs], RB.at[at, rs], dx=way)

    def second_free(k):
        at, rs, way = (0, hi, 3) if k == 1 else (2, lo, 1)
        ra[at, 0] = send(QA.at[k, rs], RA.at[at, rs], dy=way)
        rb[at, 0] = send(QB.at[k, rs], RB.at[at, rs], dx=way)

    def second_late(k):
        at, rs, way = (0, lo, 3) if k == 1 else (2, hi, 1)
        ra[k].wait_recv()
        QA[k, rs] = QA[k, rs] + RA[k, rs]
        ra[at, 1] = send(QA.at[k, rs], RA.at[at, rs], dy=way)
        rb[k].wait_recv()
        QB[k, rs] = QB[k, rs] + RB[k, rs]
        rb[at, 1] = send(QB.at[k, rs], RB.at[at, rs], dx=way)

    mine = place()
    sizes = (NX, NY, NZ, 2)
    names = ("dx", "dy", "dz", "dc")
    stages = {}

    def sums_start(stage, value):
        S[stage, mine[stage]] = value
        at = S.at[stage, mine[stage]]
        stages[stage] = [send(at, at, **{names[stage]: d}) for d in range(1, sizes[stage])]

    def sums_next(stage):
        for c in stages[stage]:
            c.wait_recv()
        value = S[stage, 0]
        for k in range(1, sizes[stage]):
            value = value + S[stage, k]
        return value

    image_part(2, 2)
    part_to_sibling(0, 2)
    image_part(2, 2, 2)
    part_to_sibling(0, 2, 2)
    text_part(2)
    plane_first()
    image_part(0)
    part[0, 0].wait_recv()
    chain("l", 4, 0)
    chain("r", 4, 1)
    chain("l", 3, 1)
    part[0, 2].wait_recv()
    chain("r", 5, 0)
    text_part(1)
    plane_next(1, False)
    text_part(3)
    plane_next(3, False)

    own, cols = IMAGE_AT[0] * ROWS, CHUNK_AT[0] * QUAD
    t2, l2, p, r, _ = pair_terms(
        dot_nt(I[own : own + ROWS, :], T[cols : cols + QUAD, :]), scale2, offset2
    )
    i = lax.broadcasted_iota(jnp.int32, (ROWS, QUAD), 0)
    j = lax.broadcasted_iota(jnp.int32, (ROWS, QUAD), 1)
    same = j == jnp.where(i < HALF, i, i + (QUAD // 2 - HALF))
    pair[own : own + ROWS, cols : cols + QUAD] = jnp.where(same, -r, p).astype(bf16)
    acc[0] -= fold(jnp.where(same, l2 * LN2, 0.0))
    acc[1] -= fold(jnp.where(same, 1.0, 0.0))
    acc[2] -= fold(jnp.where(same, t2, 0.0))

    row = lax.broadcasted_iota(jnp.int32, (8, 128), 0)
    lanes = [jnp.sum(acc[k], axis=0, keepdims=True) for k in range(3)]
    sums_start(0, jnp.where(row == 0, lanes[0], jnp.where(row == 1, lanes[1], lanes[2])))
    chain("l", 3, 0)
    chain("r", 5, 1)
    image_part(3)
    part_to_sibling(1)
    plane_next(1, True)
    plane_next(3, True)
    chain("l", 2, 1)
    image_part(1)
    part[1, 0].wait_recv()
    chain("r", 6, 0)
    sums_start(1, sums_next(0))
    chain("l", 2, 0)
    chain("r", 6, 1)
    text_part(0)
    chain("l", 1, 1)
    chain("r", 7, 0)
    plane_sum(2)
    second_far()
    sums_start(2, sums_next(1))
    plane_sum(1)
    second_free(1)
    plane_sum(3)
    second_free(3)
    plane_sum(0)
    chain("l", 1, 0)
    chain("r", 7, 1)
    second_late(1)
    second_late(3)
    sums_start(3, sums_next(2))
    total = sums_next(3)
    sums_ref[...] = jnp.broadcast_to(jnp.sum(total, axis=1, keepdims=True), (8, 128))
    for k in (0, 2):
        for n in (0, 1):
            ra[k, n].wait_recv()
            rb[k, n].wait_recv()
    dtxt_ref[:HALF] = QA[0] + (RA[0] + RA[2])
    dtxt_ref[HALF:] = QB[0] + (RB[0] + RB[2])
    for h in (0, 1):
        zl[0, h][0].wait_recv()
        zr[0, h][0].wait_recv()
    rs = img(0)
    dimg_ref[...] = PI[rs, :] + SI[rs, :] + (ZL[rs, :] + ZR[rs, :])
    for c in sent:
        c.wait_send()


def finish(
    logt_ref, sums_ref, img_ref, txt_ref, dimg_ref, dtxt_ref,
    loss_ref, gimg_ref, gtxt_ref, gtemp_ref, gbias_ref,
):
    scale = jnp.exp(logt_ref[...].reshape(1, 1))
    for ref, dref, out in ((img_ref, dimg_ref, gimg_ref), (txt_ref, dtxt_ref, gtxt_ref)):
        v = ref[...]
        inverse = lax.rsqrt(jnp.sum(v * v, axis=1, keepdims=True) + EPS)
        unit = v * inverse
        direction = dref[...] * scale
        along = jnp.sum(unit * direction, axis=1, keepdims=True)
        out[...] = inverse * (direction - unit * along)
    loss_ref[...] = sums_ref[0, 0:1] * (1.0 / TOTAL)
    gbias_ref[...] = sums_ref[1, 0:1] * (1.0 / TOTAL)
    gtemp_ref[...] = sums_ref[2, 0:1] * (LN2 / TOTAL)


def on_device(image_embed, text_embed, log_temp, bias):
    vmem = pl.BlockSpec(memory_space=pltpu.VMEM)
    hbm = pl.BlockSpec(memory_space=pltpu.HBM)
    grad = jax.ShapeDtypeStruct((ROWS, D), f32)
    one = jax.ShapeDtypeStruct((1,), f32)
    half = (HALF, D)
    dimg, dtxt, sums = pl.pallas_call(
        kernel,
        out_shape=(grad, grad, jax.ShapeDtypeStruct((8, 128), f32)),
        in_specs=[hbm, hbm, vmem, vmem],
        out_specs=(vmem,) * 3,
        scratch_shapes=[
            pltpu.SMEM((1,), f32),
            pltpu.SMEM((1,), f32),
            pltpu.VMEM((SIDE, D), bf16),
            pltpu.VMEM((SIDE, D), bf16),
            pltpu.VMEM((SIDE, SIDE), bf16),
            pltpu.VMEM((SIDE, D), f32),
            pltpu.VMEM((8 * ROWS, D), bf16),
            pltpu.VMEM((SIDE, D), f32),
            pltpu.VMEM((SIDE, D), bf16),
            pltpu.VMEM((8 * ROWS, D), f32),
            pltpu.VMEM((4, 4) + half, bf16),
            pltpu.VMEM((4, 4) + half, bf16),
            pltpu.VMEM((4,) + half, f32),
            pltpu.VMEM((4,) + half, f32),
            pltpu.VMEM((4,) + half, f32),
            pltpu.VMEM((4,) + half, f32),
            pltpu.VMEM((8 * ROWS, D), f32),
            pltpu.VMEM((8 * ROWS, D), f32),
            pltpu.VMEM((8 * ROWS, D), bf16),
            pltpu.VMEM((8 * ROWS, D), bf16),
            pltpu.VMEM((3, 8, 128), f32),
            pltpu.VMEM((4, 8, 8, 128), f32),
            pltpu.SemaphoreType.DMA((2,)),
            pltpu.SemaphoreType.DMA((NSEM,)),
            pltpu.SemaphoreType.DMA((NSEM,)),
        ],
        compiler_params=pltpu.CompilerParams(
            collective_id=0, has_side_effects=True, vmem_limit_bytes=52 * 2**20
        ),
    )(log_temp, bias, image_embed, text_embed)
    return pl.pallas_call(
        finish,
        out_shape=(one, grad, grad, one, one),
        in_specs=[vmem] * 6,
        out_specs=(vmem,) * 5,
        compiler_params=pltpu.CompilerParams(vmem_limit_bytes=16 * 2**20),
    )(log_temp, sums, image_embed, text_embed, dimg, dtxt)


def solution(mesh):
    grid = Mesh(mesh.devices.reshape(NX, NY // 2, NZ, 2, 2), AXES)
    rows = P(AXES, None)
    return jax.shard_map(
        on_device,
        mesh=grid,
        in_specs=(rows, rows, P(), P()),
        out_specs=(P(), rows, rows, P(), P()),
        check_vma=False,
    )
```

time: 280 us -> 63.4 us (0.23)
  waiting for transfers between devices: 147 us -> 0 us
  blocking collectives: 77.1 us -> 0 us
  Pallas kernels: 0 us -> 59.4 us
  matrix products: 21 us -> 0 us
  other arithmetic: 13.7 us -> 0 us
  between operations: 15.2 us -> 1.94 us
    all_gather x2 -> x0, waiting for transfers between devices: 93.4 us -> none  [the longest x1 50.3 us: on_device(): text_all = lax.all_gather(text_low, PLANE, axis=0, tiled=True)]
    psum x1 -> x0, blocking collectives: 77.1 us -> none  [on_device(): sums = lax.psum(jnp.stack([loss_sum, temp_sum, bias_sum]), AXES)]
    pallas_call x0 -> x2, Pallas kernels: none -> 59.4 us  [the longest x1 58.3 us: on_device(): pl.pallas_call(kernel, out_shape=(grad, grad, jax.ShapeDtypeStruct((8, 12...]
    reduce_scatter x2 -> x0, waiting for transfers between devices: 53.3 us -> none  [the longest x1 53.3 us: on_device(): lax.psum_scatter(image_dir, COLUMN, scatter_dimension=0, tiled=True)]
    dot_general x3 -> x0, matrix products: 21 us -> none  [the longest x1 9.74 us: pair_tile(): lax.dot_general(rows_low, text_all, (((1,), (1,)), ((), ())), preferred_e...]
    reduce_sum x4 -> x0, other arithmetic: 4.51 us -> none  [the longest x2 2.35 us: back_rows(): along = jnp.sum(unit * direction, axis=1, keepdims=True)]
    mul x2 -> x0, other arithmetic: 3.6 us -> none  [back_rows(): return inverse * (direction - unit * along)]
    convert_element_type x2 -> x0, other arithmetic: 3.44 us -> none  [the longest x1 1.72 us: on_device(): image_low = image_unit.astype(jnp.bfloat16)]
  transfers between devices with their start and end apart: 4 -> 0, of which waited for: 3 -> 0; matrix products, arithmetic and copies ran while one was open for 5% -> 0% of each run, Pallas kernels for 0% -> 0%
where the time goes in v3:
time: 63.4 us; the launch traced here: 63.2 us
  Pallas kernels  59.4 us (94%)
  between operations  1.94 us (3%)
  local copies, waits for them, and re-layouts  1.92 us (3%)
    pallas_call x1, Pallas kernels, on_device(): pl.pallas_call(kernel, out_shape=(grad, grad, jax.ShapeDtypeStruct((8, 12...  58.3 us
    unnamed x4, local copies, waits for them, and re-layouts  1.92 us

profile of v3, /device:TPU:1, one launch (start us, length us, event | category | flops | bytes accessed | tf_op | source)
XLA Modules:
  0.0 63.2 jit_solution(3730371676063282340)
XLA Ops:
  1.9 0.0 copy-start
  1.9 1.0 %copy-done = f32[64,1152]{1,0:T(8,128)S(1)} copy-done((f32[64,1152]{1,0:T(8,128)S(1)}, f32[64,1152]{1,0:T(8,128)}, u32[]{:S(2)}) %copy-start) | copy-done | bytes 294936
  2.9 0.0 copy-start.1
  2.9 1.0 %copy-done.1 = f32[64,1152]{1,0:T(8,128)S(1)} copy-done((f32[64,1152]{1,0:T(8,128)S(1)}, f32[64,1152]{1,0:T(8,128)}, u32[]{:S(2)}) %copy-start.1) | copy-done | bytes 294936
  3.8 58.3 %shard_map.83 = (f32[64,1152]{1,0:T(8,128)S(1)}, f32[64,1152]{1,0:T(8,128)S(1)}, f32[8,128]{1,0:T(8,128)S(1)}) custom-call(f32[1]{0:T(128)S(6)} %copy.9.logt_hbm.logt_ref, f32[1]{0:T(128)S(6)} %copy.10.bias_hbm, f32[64,1152]{1,0:T(8,128)S(1)} %copy-done, f32[64,1152]{1,0:T(8,128)S(1)} %copy-done.1), custom_call_target="tpu_custom_call" | custom-call | tf_op jit(solution)/shard_map/pallas_call | solution.py:478
  62.2 1.1 %shard_map.84 = (f32[1]{0:T(128)}, f32[64,1152]{1,0:T(8,128)}, f32[64,1152]{1,0:T(8,128)}, f32[1]{0:T(128)}, f32[1]{0:T(128)}) custom-call(f32[1]{0:T(128)S(6)} %copy.9.logt_hbm.logt_ref, f32[8,128]{1,0:T(8,128)S(1)} %get-tuple-element.8.sums_ref, f32[64,1152]{1,0:T(8,128)S(1)} %copy-done, f32[64,1152]{1,0:T(8,128)S(1)} %copy-done.1, ...), custom_call_target="tpu_custom_call" | custom-call | tf_op jit(solution)/shard_map/pallas_call | solution.py:514
Async XLA Ops:
  1.9 1.0 %copy-start = (f32[64,1152]{1,0:T(8,128)S(1)}, f32[64,1152]{1,0:T(8,128)}, u32[]{:S(2)}) copy-start(f32[64,1152]{1,0:T(8,128)} %img_ref.3) | copy-start | bytes 884740
  2.9 1.0 %copy-start.1 = (f32[64,1152]{1,0:T(8,128)S(1)}, f32[64,1152]{1,0:T(8,128)}, u32[]{:S(2)}) copy-start(f32[64,1152]{1,0:T(8,128)} %txt_ref.3) | copy-start | bytes 884740

commit v4 on v3

--- a/solution.py
+++ b/solution.py
@@ -19,8 +19,8 @@
 SIDE = 16 * ROWS
 QUAD = 4 * ROWS
 TOTAL = 256 * ROWS
-NARROW_HOPS = 2
-NSEM = 160
+NARROW_HOPS = {4: 2, 3: 2}
+NSEM = 192
 f32, bf16 = jnp.float32, jnp.bfloat16
 
 IMAGE_AT = {4: 0, 3: 1, 5: 2, 2: 3, 6: 4, 1: 5, 7: 6, 0: 7}
@@ -228,6 +228,19 @@
     ring(4, 2, 3)
     arrived(0)
     piece(1, 0)
+
+    own, cols = IMAGE_AT[0] * ROWS, CHUNK_AT[0] * QUAD
+    t2, l2, p, r, _ = pair_terms(
+        dot_nt(I[own : own + ROWS, :], T[cols : cols + QUAD, :]), scale2, offset2
+    )
+    i = lax.broadcasted_iota(jnp.int32, (ROWS, QUAD), 0)
+    j = lax.broadcasted_iota(jnp.int32, (ROWS, QUAD), 1)
+    same = j == jnp.where(i < HALF, i, i + (QUAD // 2 - HALF))
+    pair[own : own + ROWS, cols : cols + QUAD] = jnp.where(same, -r, p).astype(bf16)
+    acc[0] -= fold(jnp.where(same, l2 * LN2, 0.0))
+    acc[1] -= fold(jnp.where(same, 1.0, 0.0))
+    acc[2] -= fold(jnp.where(same, t2, 0.0))
+
     for q in (2, 3):
         right[3, q].wait_recv()
         left[3, q - 2].wait_recv()
@@ -281,27 +294,31 @@
 
     zl, zr = {}, {}
 
-    def chain(way, slot, h):
-        hops, got, far_buf, low_buf = (
-            (zl, zl.get((slot, h)), ZL, ZLb) if way == "l" else (zr, zr.get((slot, h)), ZR, ZRb)
-        )
-        rs = img(slot, h)
+    def chain_one(way, slot, q):
+        hops, far_buf, low_buf = (zl, ZL, ZLb) if way == "l" else (zr, ZR, ZRb)
+        narrow = NARROW_HOPS[4 if (q < 2) == (way == "l") else 3]
+        rs = quarter(slot, q)
         v = PI[rs, :] + SI[rs, :]
         hop = 1
-        if got is not None:
-            copy, hop = got
+        if (slot, q) in hops:
+            copy, hop = hops[slot, q]
             copy.wait_recv()
-            v = v + (low_buf if hop <= NARROW_HOPS else far_buf)[rs, :].astype(f32)
+            v = v + (low_buf if hop <= narrow else far_buf)[rs, :].astype(f32)
             hop += 1
         nxt = slot - 1 if way == "l" else (slot + 1) % 8
         to = NZ - 1 if way == "l" else 1
-        if hop <= NARROW_HOPS:
+        if hop <= narrow:
             PIb[rs, :] = v.astype(bf16)
-            c = send(PIb.at[rs], low_buf.at[img(nxt, h)], dz=to)
+            c = send(PIb.at[rs], low_buf.at[quarter(nxt, q)], dz=to)
         else:
             PI[rs, :] = v
-            c = send(PI.at[rs], far_buf.at[img(nxt, h)], dz=to)
-        hops[nxt, h] = (c, hop)
+            c = send(PI.at[rs], far_buf.at[quarter(nxt, q)], dz=to)
+        hops[nxt, q] = (c, hop)
+
+    def chain(distance, half):
+        for k in (0, 1):
+            chain_one("l", distance, 2 * half + k)
+            chain_one("r", 8 - distance, 2 * (1 - half) + k)
 
     xa, xb = {}, {}
 
@@ -355,9 +372,10 @@
         QB[k, rs] = QB[k, rs] + RB[k, rs]
         rb[at, 1] = send(QB.at[k, rs], RB.at[at, rs], dx=way)
 
-    mine = place()
-    sizes = (NX, NY, NZ, 2)
-    names = ("dx", "dy", "dz", "dc")
+    x, y, z, core = place()
+    mine = (core, z, x, y)
+    sizes = (2, NZ, NX, NY)
+    names = ("dc", "dz", "dx", "dy")
     stages = {}
 
     def sums_start(stage, value):
@@ -373,81 +391,61 @@
             value = value + S[stage, k]
         return value
 
+    row = lax.broadcasted_iota(jnp.int32, (8, 128), 0)
+    lanes = [jnp.sum(acc[k], axis=0, keepdims=True) for k in range(3)]
+    sums_start(0, jnp.where(row == 0, lanes[0], jnp.where(row == 1, lanes[1], lanes[2])))
     image_part(2, 2)
     part_to_sibling(0, 2)
     image_part(2, 2, 2)
     part_to_sibling(0, 2, 2)
     text_part(2)
+    sums_start(1, sums_next(0))
     plane_first()
     image_part(0)
+    image_part(3)
+    part_to_sibling(1)
     part[0, 0].wait_recv()
-    chain("l", 4, 0)
-    chain("r", 4, 1)
-    chain("l", 3, 1)
+    chain(4, 0)
     part[0, 2].wait_recv()
-    chain("r", 5, 0)
+    chain(3, 1)
     text_part(1)
     plane_next(1, False)
+    image_part(1)
     text_part(3)
     plane_next(3, False)
-
-    own, cols = IMAGE_AT[0] * ROWS, CHUNK_AT[0] * QUAD
-    t2, l2, p, r, _ = pair_terms(
-        dot_nt(I[own : own + ROWS, :], T[cols : cols + QUAD, :]), scale2, offset2
-    )
-    i = lax.broadcasted_iota(jnp.int32, (ROWS, QUAD), 0)
-    j = lax.broadcasted_iota(jnp.int32, (ROWS, QUAD), 1)
-    same = j == jnp.where(i < HALF, i, i + (QUAD // 2 - HALF))
-    pair[own : own + ROWS, cols : cols + QUAD] = jnp.where(same, -r, p).astype(bf16)
-    acc[0] -= fold(jnp.where(same, l2 * LN2, 0.0))
-    acc[1] -= fold(jnp.where(same, 1.0, 0.0))
-    acc[2] -= fold(jnp.where(same, t2, 0.0))
-
-    row = lax.broadcasted_iota(jnp.int32, (8, 128), 0)
-    lanes = [jnp.sum(acc[k], axis=0, keepdims=True) for k in range(3)]
-    sums_start(0, jnp.where(row == 0, lanes[0], jnp.where(row == 1, lanes[1], lanes[2])))
-    chain("l", 3, 0)
-    chain("r", 5, 1)
-    image_part(3)
-    part_to_sibling(1)
+    chain(3, 0)
     plane_next(1, True)
     plane_next(3, True)
-    chain("l", 2, 1)
-    image_part(1)
+    sums_start(2, sums_next(1))
+    text_part(0)
     part[1, 0].wait_recv()
-    chain("r", 6, 0)
-    sums_start(1, sums_next(0))
-    chain("l", 2, 0)
-    chain("r", 6, 1)
-    text_part(0)
-    chain("l", 1, 1)
-    chain("r", 7, 0)
+    chain(2, 1)
+    chain(2, 0)
+    chain(1, 1)
     plane_sum(2)
     second_far()
-    sums_start(2, sums_next(1))
+    sums_start(3, sums_next(2))
     plane_sum(1)
     second_free(1)
     plane_sum(3)
     second_free(3)
+    chain(1, 0)
     plane_sum(0)
-    chain("l", 1, 0)
-    chain("r", 7, 1)
     second_late(1)
     second_late(3)
-    sums_start(3, sums_next(2))
-    total = sums_next(3)
-    sums_ref[...] = jnp.broadcast_to(jnp.sum(total, axis=1, keepdims=True), (8, 128))
     for k in (0, 2):
         for n in (0, 1):
             ra[k, n].wait_recv()
             rb[k, n].wait_recv()
     dtxt_ref[:HALF] = QA[0] + (RA[0] + RA[2])
     dtxt_ref[HALF:] = QB[0] + (RB[0] + RB[2])
-    for h in (0, 1):
-        zl[0, h][0].wait_recv()
-        zr[0, h][0].wait_recv()
+    for q in range(4):
+        zl[0, q][0].wait_recv()
+        zr[0, q][0].wait_recv()
     rs = img(0)
     dimg_ref[...] = PI[rs, :] + SI[rs, :] + (ZL[rs, :] + ZR[rs, :])
+    total = sums_next(3)
+    sums_ref[...] = jnp.broadcast_to(jnp.sum(total, axis=1, keepdims=True), (8, 128))
     for c in sent:
         c.wait_send()
 

time: 63.4 us -> 61 us (0.962); the launches traced: 63.2 us -> 60.2 us
  Pallas kernels: 59.4 us -> 56.3 us
    pallas_call x1, Pallas kernels: 58.3 us -> 55.2 us  [on_device(): pl.pallas_call(kernel, out_shape=(grad, grad, jax.ShapeDtypeStruct((8, 12...]
where the time goes in v4:
time: 61 us; the launch traced here: 60.2 us
  Pallas kernels  56.3 us (92%)
  between operations  1.94 us (3%)
  local copies, waits for them, and re-layouts  1.92 us (3%)
    pallas_call x1, Pallas kernels, on_device(): pl.pallas_call(kernel, out_shape=(grad, grad, jax.ShapeDtypeStruct((8, 12...  55.2 us
    unnamed x4, local copies, waits for them, and re-layouts  1.92 us

profile of v4, /device:TPU:1, one launch (start us, length us, event | category | flops | bytes accessed | tf_op | source)
XLA Modules:
  0.0 60.2 jit_solution(17421829724161756098)
XLA Ops:
  1.9 0.0 copy-start
  1.9 1.0 %copy-done = f32[64,1152]{1,0:T(8,128)S(1)} copy-done((f32[64,1152]{1,0:T(8,128)S(1)}, f32[64,1152]{1,0:T(8,128)}, u32[]{:S(2)}) %copy-start) | copy-done | bytes 294936
  2.9 0.0 copy-start.1
  2.9 1.0 %copy-done.1 = f32[64,1152]{1,0:T(8,128)S(1)} copy-done((f32[64,1152]{1,0:T(8,128)S(1)}, f32[64,1152]{1,0:T(8,128)}, u32[]{:S(2)}) %copy-start.1) | copy-done | bytes 294936
  3.8 55.2 %shard_map.83 = (f32[64,1152]{1,0:T(8,128)S(1)}, f32[64,1152]{1,0:T(8,128)S(1)}, f32[8,128]{1,0:T(8,128)S(1)}) custom-call(f32[1]{0:T(128)S(6)} %copy.9.logt_hbm.logt_ref, f32[1]{0:T(128)S(6)} %copy.10.bias_hbm, f32[64,1152]{1,0:T(8,128)S(1)} %copy-done, f32[64,1152]{1,0:T(8,128)S(1)} %copy-done.1), custom_call_target="tpu_custom_call" | custom-call | tf_op jit(solution)/shard_map/pallas_call | solution.py:476
  59.1 1.1 %shard_map.84 = (f32[1]{0:T(128)}, f32[64,1152]{1,0:T(8,128)}, f32[64,1152]{1,0:T(8,128)}, f32[1]{0:T(128)}, f32[1]{0:T(128)}) custom-call(f32[1]{0:T(128)S(6)} %copy.9.logt_hbm.logt_ref, f32[8,128]{1,0:T(8,128)S(1)} %get-tuple-element.8.sums_ref, f32[64,1152]{1,0:T(8,128)S(1)} %copy-done, f32[64,1152]{1,0:T(8,128)S(1)} %copy-done.1, ...), custom_call_target="tpu_custom_call" | custom-call | tf_op jit(solution)/shard_map/pallas_call | solution.py:512
Async XLA Ops:
  1.9 1.0 %copy-start = (f32[64,1152]{1,0:T(8,128)S(1)}, f32[64,1152]{1,0:T(8,128)}, u32[]{:S(2)}) copy-start(f32[64,1152]{1,0:T(8,128)} %img_ref.3) | copy-start | bytes 884740
  2.9 1.0 %copy-start.1 = (f32[64,1152]{1,0:T(8,128)S(1)}, f32[64,1152]{1,0:T(8,128)}, u32[]{:S(2)}) copy-start(f32[64,1152]{1,0:T(8,128)} %txt_ref.3) | copy-start | bytes 884740

commit v5 on v4

--- a/solution.py
+++ b/solution.py
@@ -29,7 +29,7 @@
 PEERS = (
     [dict(dx=d) for d in (1, 2, 3)]
     + [dict(dy=d) for d in (1, 2, 3)]
-    + [dict(dz=d) for d in range(1, NZ)]
+    + [dict(dz=d) for d in (1, NZ - 1)]
     + [dict(dc=1)]
 )
 
@@ -249,13 +249,13 @@
     for k in (0, 1, 7, 2, 6):
         sib[k].wait_recv()
     piece(3, 0)
+    arrived(1)
+    piece(1, 1)
+    piece(3, 1)
     for q in (0, 1):
         right[4, q].wait_recv()
         left[4, q + 2].wait_recv()
     to_sibling(4)
-    arrived(1)
-    piece(1, 1)
-    piece(3, 1)
     piece(0, 0)
     piece(0, 1)
     arrived(3)
@@ -402,12 +402,12 @@
     sums_start(1, sums_next(0))
     plane_first()
     image_part(0)
-    image_part(3)
-    part_to_sibling(1)
     part[0, 0].wait_recv()
     chain(4, 0)
     part[0, 2].wait_recv()
     chain(3, 1)
+    image_part(3)
+    part_to_sibling(1)
     text_part(1)
     plane_next(1, False)
     image_part(1)
@@ -421,18 +421,18 @@
     part[1, 0].wait_recv()
     chain(2, 1)
     chain(2, 0)
-    chain(1, 1)
     plane_sum(2)
     second_far()
+    chain(1, 1)
     sums_start(3, sums_next(2))
     plane_sum(1)
     second_free(1)
     plane_sum(3)
     second_free(3)
     chain(1, 0)
-    plane_sum(0)
     second_late(1)
     second_late(3)
+    plane_sum(0)
     for k in (0, 2):
         for n in (0, 1):
             ra[k, n].wait_recv()

time: 61 us -> 60.3 us (0.989); the launches traced: 60.2 us -> 60.1 us
  no operation moved by 1% of the time
where the time goes in v5:
time: 60.3 us; the launch traced here: 60.1 us
  Pallas kernels  56.2 us (93%)
  between operations  1.94 us (3%)
  local copies, waits for them, and re-layouts  1.92 us (3%)
    pallas_call x1, Pallas kernels, on_device(): pl.pallas_call(kernel, out_shape=(grad, grad, jax.ShapeDtypeStruct((8, 12...  55.2 us
    unnamed x4, local copies, waits for them, and re-layouts  1.92 us

profile of v5, /device:TPU:1, one launch (start us, length us, event | category | flops | bytes accessed | tf_op | source)
XLA Modules:
  0.0 60.1 jit_solution(17119204464758033930)
XLA Ops:
  1.9 0.0 copy-start
  1.9 1.0 %copy-done = f32[64,1152]{1,0:T(8,128)S(1)} copy-done((f32[64,1152]{1,0:T(8,128)S(1)}, f32[64,1152]{1,0:T(8,128)}, u32[]{:S(2)}) %copy-start) | copy-done | bytes 294936
  2.9 0.0 copy-start.1
  2.9 1.0 %copy-done.1 = f32[64,1152]{1,0:T(8,128)S(1)} copy-done((f32[64,1152]{1,0:T(8,128)S(1)}, f32[64,1152]{1,0:T(8,128)}, u32[]{:S(2)}) %copy-start.1) | copy-done | bytes 294936
  3.8 55.2 %shard_map.83 = (f32[64,1152]{1,0:T(8,128)S(1)}, f32[64,1152]{1,0:T(8,128)S(1)}, f32[8,128]{1,0:T(8,128)S(1)}) custom-call(f32[1]{0:T(128)S(6)} %copy.9.logt_hbm.logt_ref, f32[1]{0:T(128)S(6)} %copy.10.bias_hbm, f32[64,1152]{1,0:T(8,128)S(1)} %copy-done, f32[64,1152]{1,0:T(8,128)S(1)} %copy-done.1), custom_call_target="tpu_custom_call" | custom-call | tf_op jit(solution)/shard_map/pallas_call | solution.py:476
  59.0 1.1 %shard_map.84 = (f32[1]{0:T(128)}, f32[64,1152]{1,0:T(8,128)}, f32[64,1152]{1,0:T(8,128)}, f32[1]{0:T(128)}, f32[1]{0:T(128)}) custom-call(f32[1]{0:T(128)S(6)} %copy.9.logt_hbm.logt_ref, f32[8,128]{1,0:T(8,128)S(1)} %get-tuple-element.8.sums_ref, f32[64,1152]{1,0:T(8,128)S(1)} %copy-done, f32[64,1152]{1,0:T(8,128)S(1)} %copy-done.1, ...), custom_call_target="tpu_custom_call" | custom-call | tf_op jit(solution)/shard_map/pallas_call | solution.py:512
Async XLA Ops:
  1.9 1.0 %copy-start = (f32[64,1152]{1,0:T(8,128)S(1)}, f32[64,1152]{1,0:T(8,128)}, u32[]{:S(2)}) copy-start(f32[64,1152]{1,0:T(8,128)} %img_ref.3) | copy-start | bytes 884740
  2.9 1.0 %copy-start.1 = (f32[64,1152]{1,0:T(8,128)S(1)}, f32[64,1152]{1,0:T(8,128)}, u32[]{:S(2)}) copy-start(f32[64,1152]{1,0:T(8,128)} %txt_ref.3) | copy-start | bytes 884740

commit v6 on v5

--- a/solution.py
+++ b/solution.py
@@ -129,7 +129,6 @@
     low = unit_low(txt_ref)
     T[ta(0, 0), :] = low[:HALF]
     T[tb(0, 0), :] = low[HALF:]
-    I[img(0), :] = unit_low(img_ref)
     pl.semaphore_wait(barrier, len(PEERS))
 
     right, left, first, near, far, sib = {}, {}, {}, {}, {}, {}
@@ -198,6 +197,7 @@
         first["b", d].wait_recv()
 
     first_send(1, 3)
+    I[img(0), :] = unit_low(img_ref)
     ring(1, 0, 1, 2, 3)
     forward(0)
     first_send(2)

time: 60.3 us -> 60.3 us (level)
  no operation moved by 1% of the time
where the time goes in v6:
time: 60.3 us; the launch traced here: 60.1 us
  Pallas kernels  56.2 us (93%)
  between operations  1.94 us (3%)
  local copies, waits for them, and re-layouts  1.92 us (3%)
    pallas_call x1, Pallas kernels, on_device(): pl.pallas_call(kernel, out_shape=(grad, grad, jax.ShapeDtypeStruct((8, 12...  55.2 us
    unnamed x4, local copies, waits for them, and re-layouts  1.92 us

profile of v6, /device:TPU:1, one launch (start us, length us, event | category | flops | bytes accessed | tf_op | source)
XLA Modules:
  0.0 60.1 jit_solution(17273520531161192468)
XLA Ops:
  1.9 0.0 copy-start
  1.9 1.0 %copy-done = f32[64,1152]{1,0:T(8,128)S(1)} copy-done((f32[64,1152]{1,0:T(8,128)S(1)}, f32[64,1152]{1,0:T(8,128)}, u32[]{:S(2)}) %copy-start) | copy-done | bytes 294936
  2.9 0.0 copy-start.1
  2.9 1.0 %copy-done.1 = f32[64,1152]{1,0:T(8,128)S(1)} copy-done((f32[64,1152]{1,0:T(8,128)S(1)}, f32[64,1152]{1,0:T(8,128)}, u32[]{:S(2)}) %copy-start.1) | copy-done | bytes 294936
  3.8 55.2 %shard_map.83 = (f32[64,1152]{1,0:T(8,128)S(1)}, f32[64,1152]{1,0:T(8,128)S(1)}, f32[8,128]{1,0:T(8,128)S(1)}) custom-call(f32[1]{0:T(128)S(6)} %copy.9.logt_hbm.logt_ref, f32[1]{0:T(128)S(6)} %copy.10.bias_hbm, f32[64,1152]{1,0:T(8,128)S(1)} %copy-done, f32[64,1152]{1,0:T(8,128)S(1)} %copy-done.1), custom_call_target="tpu_custom_call" | custom-call | tf_op jit(solution)/shard_map/pallas_call | solution.py:476
  59.0 1.1 %shard_map.84 = (f32[1]{0:T(128)}, f32[64,1152]{1,0:T(8,128)}, f32[64,1152]{1,0:T(8,128)}, f32[1]{0:T(128)}, f32[1]{0:T(128)}) custom-call(f32[1]{0:T(128)S(6)} %copy.9.logt_hbm.logt_ref, f32[8,128]{1,0:T(8,128)S(1)} %get-tuple-element.8.sums_ref, f32[64,1152]{1,0:T(8,128)S(1)} %copy-done, f32[64,1152]{1,0:T(8,128)S(1)} %copy-done.1, ...), custom_call_target="tpu_custom_call" | custom-call | tf_op jit(solution)/shard_map/pallas_call | solution.py:512
Async XLA Ops:
  1.9 1.0 %copy-start = (f32[64,1152]{1,0:T(8,128)S(1)}, f32[64,1152]{1,0:T(8,128)}, u32[]{:S(2)}) copy-start(f32[64,1152]{1,0:T(8,128)} %img_ref.3) | copy-start | bytes 884740
  2.9 1.0 %copy-start.1 = (f32[64,1152]{1,0:T(8,128)S(1)}, f32[64,1152]{1,0:T(8,128)}, u32[]{:S(2)}) copy-start(f32[64,1152]{1,0:T(8,128)} %txt_ref.3) | copy-start | bytes 884740
